TPU v7x, 32 devices: a whole 2x2x4 slice. The times are simulated.
32 devices in a mesh: group: 4 (over y, core), sub: 8 (over z, x).
Axes of the slice: x: 2, y: 2, z: 4, core: 2. Of those that a mesh axis runs over, the one named last changes fastest.
Arguments:
- right_side: float32 [16384, 128], P(('group', 'sub')), may hold values from -6 to 6
- mass: float32 [32, 512], P(('group', 'sub')), may hold values from 0.05 to 0.5
- block_values: float32 [16384, 512], P(('group', 'sub')), may hold values from 0.000390625 to 0.005859375
- block_cols: int32 [256, 8], P(('group', 'sub')), may hold values from 0 to 7, as said below
- face_rows: int32 [32, 64], P(('group', 'sub')), may hold values from 0 to 511, as said below
- land_rows: int32 [32, 64], P(('group', 'sub')), may hold values from 0 to 511, as said below
- face_counts: int32 [32, 8], P(('group', 'sub')), may hold values from 0 to 8, as said below
- face_weight: float32 [32, 64], P(('group', 'sub')), may hold values from 0.3 to 3
- local_factor: float32 [16384, 128], P(('group', 'sub')), may hold values from -0.25 to 0.25
- basis: float32 [2048, 512], P(('group', 'sub')), may hold values from -0.25 to 0.25
- coarse_inverse: float32 [512, 512], P('sub'), may hold values from -1 to 2.5, as said below
Outputs:
- solution_field: float32 [16384, 128], P(('group', 'sub'))
- residual: float32 [16384, 128], P(('group', 'sub'))
Inputs may be any that keep to these rules, and one draw needn't show every extreme that they name: `block_cols`: for each k, the column blocks of a subdomain's 8 block rows are a permutation of 0 to 7. `face_rows`: the 64 entries of a subdomain are distinct local rows. `land_rows`: the 64 entries of a subdomain are distinct local rows. `face_counts`: every subdomain has 8 live slots toward at least one peer. `coarse_inverse`: symmetric positive definite.
All inputs are finite; a program needn't handle non-finite values.
Results may differ from a plain program's by a relative error of at most 0.0003.
Values sent between devices are 32-bit elements; how exact they have to be, the bound alone decides.
A program may use at most 64 MiB of HBM per device.

v0:
```python
import jax
import jax.numpy as jnp
from jax import lax
from jax.sharding import PartitionSpec as P

ITERS = 3


highest = lax.Precision.HIGHEST


def local(
    right_side,
    mass,
    block_values,
    block_cols,
    face_rows,
    land_rows,
    face_counts,
    face_weight,
    local_factor,
    basis,
    coarse_inverse,
):
    n_rows, n_rhs = right_side.shape
    n_peers = lax.axis_size("sub")
    n_slots = face_rows.shape[1]
    per_peer = n_slots // n_peers
    n_blocks, n_stored = block_cols.shape
    block_rows = n_rows // n_blocks
    n_coarse = basis.shape[0]
    factor_rows = local_factor.shape[1]
    faces = face_rows[0]
    lands = land_rows[0]
    slot_ids = jnp.arange(n_slots)
    live = slot_ids % per_peer < face_counts[0][slot_ids // per_peer]
    weights = jnp.where(live, face_weight[0], jnp.float32(0.0))
    received = lax.all_to_all(weights, "sub", split_axis=0, concat_axis=0, tiled=True)
    values_r = block_values.reshape(n_blocks, block_rows, n_stored * block_rows)
    flat_cols = block_cols.reshape(-1)
    row_total = jnp.sum(block_values, axis=1)
    col_part = jnp.sum(values_r, axis=1).reshape(n_blocks * n_stored, block_rows)
    col_total = (
        jnp.zeros((n_blocks, block_rows), jnp.float32).at[flat_cols].add(col_part).reshape(n_rows)
    )
    degree = (row_total + col_total).at[faces].add(weights).at[lands].add(received)
    diag_col = (mass[0] + degree)[:, None]
    factor_r = local_factor.reshape(n_rows // factor_rows, factor_rows, factor_rows)

    def precondition(resid):
        jacobi = resid / diag_col
        blocks = resid.reshape(n_rows // factor_rows, factor_rows, n_rhs)
        inner = jnp.einsum("bij,bjc->bic", factor_r, blocks, precision=highest)
        local_part = jnp.einsum("bji,bjc->bic", factor_r, inner, precision=highest).reshape(
            n_rows, n_rhs
        )
        coarse_part = jnp.dot(basis, resid, precision=highest)
        total_coarse = coarse_inverse.shape[1]
        start = lax.axis_index("sub") * n_coarse
        padded = lax.dynamic_update_slice_in_dim(
            jnp.zeros((total_coarse, n_rhs), jnp.float32), coarse_part, start, 0
        )
        whole = lax.psum(padded, ("group", "sub"))
        solved = jnp.dot(coarse_inverse, whole, precision=highest)
        coarse_term = jnp.einsum("nr,nc->rc", basis, solved, precision=highest)
        return jacobi + local_part + coarse_term

    def residual_product(resid, zvalue):
        return lax.psum(jnp.sum(resid * zvalue, axis=0), ("group", "sub"))

    resid = right_side
    solution = jnp.zeros_like(right_side)
    zvalue = precondition(resid)
    direction = zvalue
    gamma = residual_product(resid, zvalue)
    for iteration in range(ITERS):
        got_out = lax.all_to_all(
            weights[:, None] * direction[faces], "sub", split_axis=0, concat_axis=0, tiled=True
        )
        got_back = lax.all_to_all(direction[lands], "sub", split_axis=0, concat_axis=0, tiled=True)
        operate_blocks = direction.reshape(n_blocks, block_rows, n_rhs)
        picked = operate_blocks[block_cols].reshape(n_blocks, n_stored * block_rows, n_rhs)
        forward = jnp.einsum("rik,rkc->ric", values_r, picked, precision=highest).reshape(
            n_rows, n_rhs
        )
        back_terms = jnp.einsum(
            "rik,ric->rkc", values_r, operate_blocks, precision=highest
        ).reshape(n_blocks * n_stored, block_rows, n_rhs)
        backward = (
            jnp.zeros((n_blocks, block_rows, n_rhs), jnp.float32)
            .at[flat_cols]
            .add(back_terms)
            .reshape(n_rows, n_rhs)
        )
        coupled = jnp.zeros((n_rows, n_rhs), jnp.float32).at[lands].add(got_out)
        coupled = coupled.at[faces].add(weights[:, None] * got_back)
        image = diag_col * direction - forward - backward - coupled
        alpha = gamma / lax.psum(jnp.sum(direction * image, axis=0), ("group", "sub"))
        solution = solution + alpha * direction
        resid = resid - alpha * image
        if iteration + 1 < ITERS:
            zvalue = precondition(resid)
            gamma_new = residual_product(resid, zvalue)
            direction = zvalue + gamma_new / gamma * direction
            gamma = gamma_new
    return (solution, resid)


def solution(mesh):
    placed = (
        P(("group", "sub"), None),
        P(("group", "sub"), None),
        P(("group", "sub"), None),
        P(("group", "sub"), None),
        P(("group", "sub"), None),
        P(("group", "sub"), None),
        P(("group", "sub"), None),
        P(("group", "sub"), None),
        P(("group", "sub"), None),
        P(("group", "sub"), None),
        P("sub", None),
    )
    return jax.shard_map(
        local,
        mesh=mesh,
        in_specs=placed,
        out_specs=(P(("group", "sub"), None), P(("group", "sub"), None)),
        check_vma=False,
    )
```

profile of v0, /device:TPU:0, one launch (start us, length us, event | category | flops | bytes accessed | tf_op | source)
XLA Modules:
  0.0 727.0 jit_solution(14743907355516807728)
XLA Ops:
  8.8 5.7 compare_select_fusion.11
  17.2 7.3 all-to-all-start
  34.9 122.8 %all-reduce.5.cloned.1.call-done = f32[512,128]{1,0:T(8,128)} async-done(((f32[512,128]{1,0:T(8,128)}), f32[512,128]{1,0:T(8,128)}) %all-reduce.5.cloned.1.call-update) | async-done | bytes 262160 | tf_op jit(solution)/shard_map/psum | solution.py:63
  160.9 4.5 all-to-all-start.1
  167.4 3.1 fusion.44
  172.0 5.7 all-to-all-start.2
  177.8 3.2 convolution_bitcast_fusion.2
  183.9 7.0 scatter_fusion.2
  193.5 40.1 %all-reduce = (f32[128]{0:T(128)S(1)}, f32[128]{0:T(128)S(1)}) all-reduce(f32[128]{0:T(128)S(1)} %get-tuple-element.9, f32[128]{0:T(128)S(1)} %get-tuple-element.8), channel_id=1, replica_groups=mesh['group'=4,'sub'=8] {'group','sub'}, use_global_device_ids=true, to_apply=%region_7.8 | all-reduce | flops 256 | bytes 2048 | tf_op jit(solution)/shard_map/psum | solution.py:69
  236.3 125.2 %all-reduce.7.cloned.1.call-done = f32[512,128]{1,0:T(8,128)} async-done(((f32[512,128]{1,0:T(8,128)}), f32[512,128]{1,0:T(8,128)}) %all-reduce.7.cloned.1.call-update) | async-done | bytes 262160 | tf_op jit(solution)/shard_map/psum | solution.py:63
  363.2 39.2 %psum.67 = f32[128]{0:T(128)S(1)} all-reduce(f32[128]{0:T(128)S(1)} %get-tuple-element.29), channel_id=1, replica_groups=mesh['group'=4,'sub'=8] {'group','sub'}, use_global_device_ids=true, to_apply=%region_15.16 | all-reduce | flops 128 | bytes 1024 | tf_op jit(solution)/shard_map/psum | solution.py:69
  406.0 5.3 all-to-all-start.3
  418.0 3.7 all-to-all-start.4
  421.7 3.2 convolution_bitcast_fusion.1
  427.8 7.0 scatter_fusion.3
  437.4 40.1 %psum.68 = f32[128]{0:T(128)S(1)} all-reduce(f32[128]{0:T(128)S(1)} %get-tuple-element.14), channel_id=1, replica_groups=mesh['group'=4,'sub'=8] {'group','sub'}, use_global_device_ids=true, to_apply=%region_20.21 | all-reduce | flops 128 | bytes 1024 | tf_op jit(solution)/shard_map/psum | solution.py:98
  480.2 125.1 %all-reduce.9.cloned.1.call-done = f32[512,128]{1,0:T(8,128)} async-done(((f32[512,128]{1,0:T(8,128)}), f32[512,128]{1,0:T(8,128)}) %all-reduce.9.cloned.1.call-update) | async-done | bytes 262160 | tf_op jit(solution)/shard_map/psum | solution.py:63
  607.1 39.2 %psum.70 = f32[128]{0:T(128)S(1)} all-reduce(f32[128]{0:T(128)S(1)} %get-tuple-element.31), channel_id=1, replica_groups=mesh['group'=4,'sub'=8] {'group','sub'}, use_global_device_ids=true, to_apply=%region_23.24 | all-reduce | flops 128 | bytes 1024 | tf_op jit(solution)/shard_map/psum | solution.py:69
  649.9 5.3 all-to-all-start.5
  655.1 3.8 fusion.50
  661.8 4.3 all-to-all-start.6
  666.1 3.2 convolution_bitcast_fusion
  671.2 3.7 scatter_fusion.4
  678.6 40.0 %psum.71 = f32[128]{0:T(128)S(1)} all-reduce(f32[128]{0:T(128)S(1)} %get-tuple-element.12), channel_id=1, replica_groups=mesh['group'=4,'sub'=8] {'group','sub'}, use_global_device_ids=true, to_apply=%region_28.29 | all-reduce | flops 128 | bytes 1024 | tf_op jit(solution)/shard_map/psum | solution.py:98
  (154 shorter events, 64.9 us)
Async XLA Ops:
  7.2 23.5 %copy-start = (f32[512,128]{1,0:T(8,128)S(1)}, f32[512,128]{1,0:T(8,128)}, u32[]{:S(2)}) copy-start(f32[512,128]{1,0:T(8,128)} %param.19) | copy-start | bytes 786436
  7.2 23.5 %copy-start.10 = (f32[512,128]{1,0:T(8,128)S(1)}, f32[512,128]{1,0:T(8,128)}, u32[]{:S(2)}) copy-start(f32[512,128]{1,0:T(8,128)} %param.11) | copy-start | bytes 786436
  7.2 23.3 %copy-start.1 = (f32[512,512]{1,0:T(8,128)S(1)}, f32[512,512]{1,0:T(8,128)}, u32[]{:S(2)}) copy-start(f32[512,512]{1,0:T(8,128)} %param.13) | copy-start | bytes 3145732
  17.2 16.0 %all-to-all-start = ((f32[8,8,1]{1,2,0:T(1,128)}), f32[8,8,1]{1,2,0:T(1,128)S(1)}, u32[]{:S(2)}, u32[]{:S(2)}) async-start(f32[8,8,1]{1,2,0:T(1,128)} %bitcast.18), calls=%async_computation | async-start | bytes 8192 | tf_op jit(solution)/shard_map/all_to_all | solution.py:38
  24.4 133.3 %all-reduce.5.cloned.1.call-start = ((), (), s32[]{:S(2)}) async-start(), calls=%async_computation.7 | async-start | bytes 524288 | tf_op jit(solution)/shard_map/psum | solution.py:63
  25.8 5.9 copy-start.18
  25.9 5.9 copy-start.17
  25.9 6.0 copy-start.16
  31.1 126.7 %copy-start.11 = (f32[64,512]{1,0:T(8,128)S(1)}, f32[64,512]{1,0:T(8,128)}, u32[]{:S(2)}) copy-start(f32[64,512]{1,0:T(8,128)} %param.21) | copy-start | bytes 393220
  31.1 128.0 %copy-start.12 = (f32[64,512]{1,0:T(8,128)S(1)}, f32[64,512]{1,0:T(8,128)}, u32[]{:S(2)}) copy-start(f32[64,512]{1,0:T(8,128)} %param.20) | copy-start | bytes 393220
  159.5 243.0 %copy-start.8 = (f32[512,128]{0,1:T(8,128)}, f32[512,128]{0,1:T(8,128)S(1)}, u32[]{:S(2)}) copy-start(f32[512,128]{0,1:T(8,128)S(1)} %fusion.2) | copy-start | bytes 786436
  160.9 11.1 %all-to-all-start.1 = ((f32[8,8,128]{2,1,0:T(8,128)}), f32[8,8,128]{2,1,0:T(8,128)S(1)}, u32[]{:S(2)}, u32[]{:S(2)}) async-start(f32[8,8,128]{2,1,0:T(8,128)} %bitcast_multiply_fusion.8), calls=%async_computation.1 | async-start | bytes 65536 | tf_op jit(solution)/shard_map/all_to_all | solution.py:77
  172.0 20.1 %all-to-all-start.2 = ((f32[8,8,128]{2,1,0:T(8,128)}), f32[8,8,128]{2,1,0:T(8,128)S(1)}, u32[]{:S(2)}, u32[]{:S(2)}) async-start(f32[8,8,128]{2,1,0:T(8,128)} %bitcast.33), calls=%async_computation.2 | async-start | bytes 65536 | tf_op jit(solution)/shard_map/all_to_all | solution.py:80
  177.7 183.7 %all-reduce.7.cloned.1.call-start = ((), (), s32[]{:S(2)}) async-start(), calls=%async_computation.8 | async-start | bytes 524288 | tf_op jit(solution)/shard_map/psum | solution.py:63
  402.6 243.8 %copy-start.2 = (f32[512,128]{0,1:T(8,128)}, f32[512,128]{0,1:T(8,128)S(1)}, u32[]{:S(2)}) copy-start(f32[512,128]{0,1:T(8,128)S(1)} %multiply_add_fusion.2) | copy-start | bytes 786436
  406.0 12.0 %all-to-all-start.3 = ((f32[8,8,128]{2,1,0:T(8,128)}), f32[8,8,128]{2,1,0:T(8,128)S(1)}, u32[]{:S(2)}, u32[]{:S(2)}) async-start(f32[8,8,128]{2,1,0:T(8,128)} %bitcast_multiply_fusion.5), calls=%async_computation.3 | async-start | bytes 65536 | tf_op jit(solution)/shard_map/all_to_all | solution.py:77
  418.0 18.0 %all-to-all-start.4 = ((f32[8,8,128]{2,1,0:T(8,128)}), f32[8,8,128]{2,1,0:T(8,128)S(1)}, u32[]{:S(2)}, u32[]{:S(2)}) async-start(f32[8,8,128]{2,1,0:T(8,128)} %bitcast.48), calls=%async_computation.4 | async-start | bytes 65536 | tf_op jit(solution)/shard_map/all_to_all | solution.py:80
  421.6 183.6 %all-reduce.9.cloned.1.call-start = ((), (), s32[]{:S(2)}) async-start(), calls=%async_computation.9 | async-start | bytes 524288 | tf_op jit(solution)/shard_map/psum | solution.py:63
  477.6 129.4 %copy-start.4 = (f32[512,128]{0,1:T(8,128)}, f32[512,128]{0,1:T(8,128)S(1)}, u32[]{:S(2)}) copy-start(f32[512,128]{0,1:T(8,128)S(1)} %multiply_subtract_fusion.1) | copy-start | bytes 786436
  649.9 12.0 %all-to-all-start.5 = ((f32[8,8,128]{2,1,0:T(8,128)}), f32[8,8,128]{2,1,0:T(8,128)S(1)}, u32[]{:S(2)}, u32[]{:S(2)}) async-start(f32[8,8,128]{2,1,0:T(8,128)} %bitcast_multiply_fusion.2), calls=%async_computation.5 | async-start | bytes 65536 | tf_op jit(solution)/shard_map/all_to_all | solution.py:77
  661.8 15.4 %all-to-all-start.6 = ((f32[8,8,128]{2,1,0:T(8,128)}), f32[8,8,128]{2,1,0:T(8,128)S(1)}, u32[]{:S(2)}, u32[]{:S(2)}) async-start(f32[8,8,128]{2,1,0:T(8,128)} %bitcast.63), calls=%async_computation.6 | async-start | bytes 65536 | tf_op jit(solution)/shard_map/all_to_all | solution.py:80
  675.0 43.6 %copy-start.3 = (f32[512,128]{0,1:T(8,128)S(1)}, f32[512,128]{0,1:T(8,128)}, u32[]{:S(2)}) copy-start(f32[512,128]{0,1:T(8,128)} %copy-done.2) | copy-start | bytes 786436
  675.0 43.6 %copy-start.5 = (f32[512,128]{0,1:T(8,128)S(1)}, f32[512,128]{0,1:T(8,128)}, u32[]{:S(2)}) copy-start(f32[512,128]{0,1:T(8,128)} %copy-done.4) | copy-start | bytes 786436
  675.0 43.6 %copy-start.9 = (f32[512,128]{0,1:T(8,128)S(1)}, f32[512,128]{0,1:T(8,128)}, u32[]{:S(2)}) copy-start(f32[512,128]{0,1:T(8,128)} %copy-done.8) | copy-start | bytes 786436
  (6 other events, 14.2 us)
Sparse Core Ops, SparseCore 0:
  31.3 126.3 all-reduce.4
  235.6 125.7 all-reduce.6
  479.6 125.6 all-reduce.8
where the time goes:
time: 729 us; the launch traced here: 727 us
  waiting for transfers between devices  378 us (52%)
  blocking collectives  199 us (27%)
  other arithmetic  40.1 us (6%)
  starting transfers between devices  36 us (5%)
  matrix products  30.5 us (4%)
  local copies, waits for them, and re-layouts  29.7 us (4%)
  between operations  14.4 us (2%)
    psum x3, waiting for transfers between devices, precondition(): whole = lax.psum(padded, ('group', 'sub'))  373 us
    psum x3, blocking collectives, residual_product(): return lax.psum(jnp.sum(resid * zvalue, axis=0), ('group', 'sub'))  119 us
    psum x2, blocking collectives, local(): lax.psum(jnp.sum(direction * image, axis=0), ('group', 'sub'))  80.1 us
    scatter-add x3, other arithmetic, local(): backward = jnp.zeros((n_blocks, block_rows, n_rhs), jnp.float32).at[flat_...  17.8 us
    all_to_all x3, starting transfers between devices, local(): lax.all_to_all(weights[:, None] * direction[faces], 'sub', split_axis=0,...  15 us
  transfers between devices with their start and end apart: 10, of which 6 were waited for; matrix products, arithmetic and copies ran while one was open for 9% of the time, Pallas kernels for 0%

commit v1 on v0

v1 whole, which is shorter than its diff:
```python
import functools

import jax
import jax.numpy as jnp
from jax import lax
from jax.experimental import pallas as pl
from jax.experimental.pallas import tpu as pltpu
from jax.sharding import PartitionSpec as P

HIGHEST = lax.Precision.HIGHEST
MESH = pl.DeviceIdType.MESH
LANES = 128
SUBLANES = 8


def mm(a, b):
    return jnp.dot(a, b, precision=HIGHEST, preferred_element_type=jnp.float32)


def stack_dots(rows):
    pad = SUBLANES - len(rows)
    return jnp.concatenate(rows + [jnp.zeros((pad, rows[0].shape[1]), jnp.float32)], axis=0)


def column_dot(a, b):
    return jnp.sum(a * b, axis=0, keepdims=True)


def kernel(
    n_group,
    n_sub,
    rs_ref,
    mass_ref,
    values_ref,
    cols_ref,
    faces_ref,
    lands_ref,
    counts_ref,
    fweight_ref,
    factor_ref,
    basis_ref,
    coarse_ref,
    x_ref,
    r_ref,
    dense,
    near,
    inv_diag,
    diag,
    basis_t,
    select,
    spread,
    extend_out,
    extend_in,
    weight_out,
    weight_in,
    group_buf,
    sub_buf,
    face_out,
    face_in,
    group_dots,
    sub_dots,
    send_sem,
    recv_sem,
):
    me_g = lax.axis_index("group")
    me_s = lax.axis_index("sub")
    n_rows, n_rhs = rs_ref.shape
    n_slots = faces_ref.shape[1]
    per_peer = n_slots // n_sub
    n_blocks, n_stored = cols_ref.shape
    block_rows = n_rows // n_blocks
    n_coarse = basis_ref.shape[0]
    total_coarse = coarse_ref.shape[1]
    factor_rows = factor_ref.shape[1]
    n_factors = n_rows // factor_rows

    barrier = pltpu.get_barrier_semaphore()
    for step in range(1, n_group):
        peer = lax.rem(me_g + step, n_group)
        pl.semaphore_signal(barrier, inc=1, device_id=(peer, me_s), device_id_type=MESH)
    for step in range(1, n_sub):
        peer = lax.rem(me_s + step, n_sub)
        pl.semaphore_signal(barrier, inc=1, device_id=(me_g, peer), device_id_type=MESH)

    pending = []

    def over_sub(channel, src_of, dst):
        for step in range(1, n_sub):
            peer = lax.rem(me_s + step, n_sub)
            pltpu.make_async_remote_copy(
                src_ref=src_of(peer),
                dst_ref=dst,
                send_sem=send_sem.at[channel],
                recv_sem=recv_sem.at[channel],
                device_id=(me_g, peer),
                device_id_type=MESH,
            ).start()

    def over_group(channel, src, dst):
        for step in range(1, n_group):
            peer = lax.rem(me_g + step, n_group)
            pltpu.make_async_remote_copy(
                src_ref=src,
                dst_ref=dst,
                send_sem=send_sem.at[channel],
                recv_sem=recv_sem.at[channel],
                device_id=(peer, me_s),
                device_id_type=MESH,
            ).start()

    def arrive(channel, buf, count):
        if count > 0:
            part = buf.at[pl.ds(0, count)]
            pltpu.make_async_copy(part, part, recv_sem.at[channel]).wait()
            pending.append((channel, buf, count))

    slot = lax.broadcasted_iota(jnp.int32, (1, n_slots), 1)
    count_row = jnp.zeros((1, n_slots), jnp.int32)
    for p in range(n_sub):
        count_row = jnp.where(slot // per_peer == p, counts_ref[0, p], count_row)
    weights = jnp.where(slot % per_peer < count_row, fweight_ref[...], jnp.float32(0.0))
    row_ids = lax.broadcasted_iota(jnp.int32, (n_rows, n_slots), 0)
    face_hot = jnp.where(row_ids == faces_ref[...], weights, jnp.float32(0.0))
    land_hot = jnp.where(row_ids == lands_ref[...], jnp.float32(1.0), jnp.float32(0.0))
    spread[:, :n_slots] = land_hot
    spread[:, n_slots:] = face_hot
    select[:n_slots, :] = face_hot.T
    select[n_slots:, :] = land_hot.T

    weight_out[...] = mm(
        select[:n_slots, :], jnp.ones((n_rows, n_rhs), jnp.float32)
    ).reshape(n_sub, per_peer, n_rhs)
    weight_in[pl.ds(me_s, 1)] = weight_out[pl.ds(me_s, 1)]
    resid = rs_ref[...]
    group_buf[0, me_g] = jnp.concatenate(
        [mm(basis_ref[...], resid), jnp.zeros((SUBLANES, n_rhs), jnp.float32)], axis=0
    )

    pl.semaphore_wait(barrier, n_group - 1 + n_sub - 1)

    over_group(2, group_buf.at[0, me_g], group_buf.at[0, me_g])
    over_sub(0, lambda peer: weight_out.at[peer], weight_in.at[me_s])

    basis_t[...] = basis_ref[...].T
    reach = mm(mm(select[...], basis_t[...]), coarse_ref[...])
    extend_out[:, :per_peer, :] = reach[:n_slots].reshape(n_sub, per_peer, total_coarse)
    extend_out[:, per_peer:, :] = reach[n_slots:].reshape(n_sub, per_peer, total_coarse)
    extend_in[pl.ds(me_s, 1)] = extend_out[pl.ds(me_s, 1)]

    def gather_group(phase):
        arrive(2 + phase, group_buf.at[phase], n_group - 1)
        total = group_buf[phase, 0]
        for g in range(1, n_group):
            total = total + group_buf[phase, g]
        sub_buf[phase, me_s] = total
        over_sub(6 + phase, lambda peer: sub_buf.at[phase, me_s], sub_buf.at[phase, me_s])

    gather_group(0)
    over_sub(1, lambda peer: extend_out.at[peer], extend_in.at[me_s])

    lane = lax.broadcasted_iota(jnp.int32, (1, LANES), 1)
    high = jnp.where(lane >= block_rows, 1, 0)
    n_tiles = n_rows // LANES
    stored_tiles = n_stored * block_rows // LANES
    for b in range(n_blocks):
        rows = slice(b * block_rows, (b + 1) * block_rows)
        sums = [jnp.zeros((block_rows, LANES), jnp.float32) for _ in range(n_tiles)]
        for t in range(stored_tiles):
            tile = values_ref[rows, t * LANES : (t + 1) * LANES]
            turned = pltpu.roll(tile, block_rows, 1)
            first, second = cols_ref[b, 2 * t], cols_ref[b, 2 * t + 1]
            straight_cols = jnp.where(high == 0, first, second)
            turned_cols = jnp.where(high == 0, second, first)
            for u in range(n_tiles):
                target = 2 * u + high
                sums[u] = (
                    sums[u]
                    + jnp.where(straight_cols == target, tile, jnp.float32(0.0))
                    + jnp.where(turned_cols == target, turned, jnp.float32(0.0))
                )
        for u in range(n_tiles):
            dense[rows, u * LANES : (u + 1) * LANES] = sums[u]
    dense[...] = dense[...] + dense[...].T

    for i in range(n_factors):
        rows = slice(i * factor_rows, (i + 1) * factor_rows)
        part = factor_ref[rows, :]
        near[rows, :] = mm(part.T, part)

    degree = mm(dense[...], jnp.ones((n_rows, n_rhs), jnp.float32))
    mass_col = jnp.broadcast_to(mass_ref[...], (n_rhs, n_rows)).T
    arrive(0, weight_in, n_sub - 1)
    degree = degree + mm(
        spread[...],
        jnp.concatenate(
            [
                weight_in[...].reshape(n_slots, n_rhs),
                jnp.ones((n_slots, n_rhs), jnp.float32),
            ],
            axis=0,
        ),
    )
    diag[...] = mass_col + degree
    inv_diag[...] = 1.0 / diag[...]

    def send_coarse(phase, field, dots):
        group_buf[phase, me_g] = jnp.concatenate([mm(basis_ref[...], field), dots], axis=0)
        over_group(2 + phase, group_buf.at[phase, me_g], group_buf.at[phase, me_g])

    def send_local(phase, field):
        parts = []
        for i in range(n_factors):
            rows = slice(i * factor_rows, (i + 1) * factor_rows)
            parts.append(mm(near[rows, :], field[rows, :]))
        local_part = field * inv_diag[...] + jnp.concatenate(parts, axis=0)
        picked = mm(select[...], local_part)
        face_out[phase, :, :per_peer, :] = picked[:n_slots].reshape(n_sub, per_peer, n_rhs)
        face_out[phase, :, per_peer:, :] = picked[n_slots:].reshape(n_sub, per_peer, n_rhs)
        face_in[phase, me_s] = face_out[phase, me_s]
        over_sub(10 + phase, lambda peer: face_out.at[phase, peer], face_in.at[phase, me_s])
        return local_part

    def receive(phase, local_part):
        arrive(6 + phase, sub_buf.at[phase], n_sub - 1)
        whole = sub_buf[phase, :, :n_coarse, :].reshape(total_coarse, n_rhs)
        dots = jnp.sum(sub_buf[phase, :, n_coarse:, :], axis=0)
        if phase == 0:
            arrive(1, extend_in, n_sub - 1)
        field = local_part + mm(basis_t[...], mm(coarse_ref[...], whole))
        far = mm(extend_in[...].reshape(2 * n_slots, total_coarse), whole)
        arrive(10 + phase, face_in.at[phase], n_sub - 1)
        far = far.reshape(n_sub, 2 * per_peer, n_rhs) + face_in[phase]
        far = jnp.concatenate(
            [
                far[:, :per_peer, :].reshape(n_slots, n_rhs),
                far[:, per_peer:, :].reshape(n_slots, n_rhs),
            ],
            axis=0,
        )
        return field, far, dots

    def operate(field, far):
        return diag[...] * field - mm(dense[...], field) - mm(spread[...], far)

    local_part = send_local(0, resid)
    z, z_far, _ = receive(0, local_part)
    image = operate(z, z_far)
    send_coarse(1, image, stack_dots([column_dot(resid, z), column_dot(z, image)]))
    local_part = send_local(1, image)
    gather_group(1)
    m_image, m_far, dots = receive(1, local_part)
    gamma, bent = dots[0:1], dots[1:2]
    alpha = gamma / bent
    direction = z
    answer = alpha * direction
    resid = resid - alpha * image
    z = z - alpha * m_image
    z_far = z_far - alpha * m_far
    z_image = operate(z, z_far)
    send_coarse(
        2,
        z_image,
        stack_dots([column_dot(resid, z), column_dot(z, z_image), column_dot(z, image)]),
    )
    local_part = send_local(2, z_image)
    gather_group(2)
    m_z_image, m_z_far, dots = receive(2, local_part)
    beta = dots[0:1] / gamma
    gamma = dots[0:1]
    bent = dots[1:2] + beta * (2.0 * dots[2:3] + beta * bent)
    alpha = gamma / bent
    direction = z + beta * direction
    image = z_image + beta * image
    answer = answer + alpha * direction
    resid = resid - alpha * image
    z = z - alpha * (m_z_image + beta * m_image)
    z_far = z_far - alpha * (m_z_far + beta * m_far)
    z_image = operate(z, z_far)
    group_dots[me_g] = stack_dots(
        [column_dot(resid, z), column_dot(z, z_image), column_dot(z, image)]
    )
    over_group(5, group_dots.at[me_g], group_dots.at[me_g])
    arrive(5, group_dots, n_group - 1)
    sub_dots[me_s] = jnp.sum(group_dots[...], axis=0)
    over_sub(9, lambda peer: sub_dots.at[me_s], sub_dots.at[me_s])
    arrive(9, sub_dots, n_sub - 1)
    dots = jnp.sum(sub_dots[...], axis=0)
    beta = dots[0:1] / gamma
    gamma = dots[0:1]
    bent = dots[1:2] + beta * (2.0 * dots[2:3] + beta * bent)
    alpha = gamma / bent
    x_ref[...] = answer + alpha * (z + beta * direction)
    r_ref[...] = resid - alpha * (z_image + beta * image)

    for channel, buf, count in pending:
        part = buf.at[pl.ds(0, count)]
        pltpu.make_async_copy(part, part, send_sem.at[channel]).wait()


def local(n_group, n_sub, *args):
    right_side, block_cols, face_rows = args[0], args[3], args[4]
    basis, coarse_inverse = args[9], args[10]
    n_rows, n_rhs = right_side.shape
    n_slots = face_rows.shape[1]
    per_peer = n_slots // n_sub
    n_coarse = basis.shape[0]
    total_coarse = coarse_inverse.shape[1]
    factor_rows = args[8].shape[1]
    f32 = jnp.float32
    vmem = pl.BlockSpec(memory_space=pltpu.VMEM)
    smem = pl.BlockSpec(memory_space=pltpu.SMEM)
    in_specs = [vmem, vmem, vmem, smem, vmem, vmem, smem, vmem, vmem, vmem, vmem]
    message = n_coarse + SUBLANES
    scratch = [
        pltpu.VMEM((n_rows, n_rows), f32),
        pltpu.VMEM((n_rows, factor_rows), f32),
        pltpu.VMEM((n_rows, n_rhs), f32),
        pltpu.VMEM((n_rows, n_rhs), f32),
        pltpu.VMEM((n_rows, n_coarse), f32),
        pltpu.VMEM((2 * n_slots, n_rows), f32),
        pltpu.VMEM((n_rows, 2 * n_slots), f32),
        pltpu.VMEM((n_sub, 2 * per_peer, total_coarse), f32),
        pltpu.VMEM((n_sub, 2 * per_peer, total_coarse), f32),
        pltpu.VMEM((n_sub, per_peer, n_rhs), f32),
        pltpu.VMEM((n_sub, per_peer, n_rhs), f32),
        pltpu.VMEM((3, n_group, message, n_rhs), f32),
        pltpu.VMEM((3, n_sub, message, n_rhs), f32),
        pltpu.VMEM((3, n_sub, 2 * per_peer, n_rhs), f32),
        pltpu.VMEM((3, n_sub, 2 * per_peer, n_rhs), f32),
        pltpu.VMEM((n_group, SUBLANES, n_rhs), f32),
        pltpu.VMEM((n_sub, SUBLANES, n_rhs), f32),
        pltpu.SemaphoreType.DMA((13,)),
        pltpu.SemaphoreType.DMA((13,)),
    ]
    field = jax.ShapeDtypeStruct((n_rows, n_rhs), f32)
    return pl.pallas_call(
        functools.partial(kernel, n_group, n_sub),
        out_shape=(field, field),
        in_specs=in_specs,
        out_specs=(vmem, vmem),
        scratch_shapes=scratch,
        compiler_params=pltpu.CompilerParams(
            collective_id=0, has_side_effects=True, vmem_limit_bytes=48 * 1024 * 1024
        ),
    )(*args)


def solution(mesh):
    n_group, n_sub = mesh.shape["group"], mesh.shape["sub"]
    rows = P(("group", "sub"), None)
    return jax.shard_map(
        functools.partial(local, n_group, n_sub),
        mesh=mesh,
        in_specs=(rows,) * 10 + (P("sub", None),),
        out_specs=(rows, rows),
        check_vma=False,
    )
```

time: 729 us -> 76.4 us (0.10)
  waiting for transfers between devices: 378 us -> 0 us
  blocking collectives: 199 us -> 0 us
  Pallas kernels: 0 us -> 65 us
  other arithmetic: 40.1 us -> 0 us
  starting transfers between devices: 36 us -> 0 us
  matrix products: 30.5 us -> 0 us
  local copies, waits for them, and re-layouts: 29.7 us -> 10.3 us
  between operations: 14.4 us -> 0.66 us
    psum x3 -> x0, waiting for transfers between devices: 373 us -> none  [precondition(): whole = lax.psum(padded, ('group', 'sub'))]
    psum x5 -> x0, blocking collectives: 199 us -> none  [the longest x3 119 us: residual_product(): return lax.psum(jnp.sum(resid * zvalue, axis=0), ('group', 'sub'))]
    pallas_call x0 -> x1, Pallas kernels: none -> 65 us  [local(): pl.pallas_call(functools.partial(kernel, n_group, n_sub), out_shape=(fiel...]
    all_to_all x7 -> x0, starting transfers between devices: 35.9 us -> none  [the longest x3 15 us: local(): lax.all_to_all(weights[:, None] * direction[faces], 'sub', split_axis=0,...]
    dot_general x21 -> x0, matrix products: 30.5 us -> none  [the longest x3 10.1 us: local(): jnp.einsum('rik,rkc->ric', values_r, picked, precision=highest)]
    scatter-add x12 -> x0, other arithmetic: 26.6 us -> none  [the longest x3 17.8 us: local(): backward = jnp.zeros((n_blocks, block_rows, n_rhs), jnp.float32).at[flat_...]
    gather x12 -> x0, local copies, waits for them, and re-layouts: 13.3 us -> none  [the longest x3 6.1 us: local(): operate_blocks[block_cols].reshape(n_blocks, n_stored * block_rows, n_rhs)]
    dot_general x3 -> x0, local copies, waits for them, and re-layouts: 7.67 us -> none  [local(): jnp.einsum('rik,ric->rkc', values_r, operate_blocks, precision=highest)]
  transfers between devices with their start and end apart: 10 -> 0, of which waited for: 6 -> 0; matrix products, arithmetic and copies ran while one was open for 9% -> 0% of each run, Pallas kernels for 0% -> 0%
where the time goes in v1:
time: 76.4 us; the launch traced here: 76 us
  Pallas kernels  65 us (85%)
  local copies, waits for them, and re-layouts  10.3 us (13%)
    pallas_call x1, Pallas kernels, local(): pl.pallas_call(functools.partial(kernel, n_group, n_sub), out_shape=(fiel...  65 us
    unnamed x24, local copies, waits for them, and re-layouts  10.3 us

profile of v1, /device:TPU:0, one launch (start us, length us, event | category | flops | bytes accessed | tf_op | source)
XLA Modules:
  0.0 76.0 jit_solution(4275314128211127303)
XLA Ops:
  0.6 0.0 copy-start
  0.6 1.2 %copy-done = f32[512,512]{1,0:T(8,128)S(1)} copy-done((f32[512,512]{1,0:T(8,128)S(1)}, f32[512,512]{1,0:T(8,128)}, u32[]{:S(2)}) %copy-start) | copy-done | bytes 1048600
  1.9 0.0 copy-start.1
  1.9 0.9 %copy-done.1 = f32[512,128]{1,0:T(8,128)S(1)} copy-done((f32[512,128]{1,0:T(8,128)S(1)}, f32[512,128]{1,0:T(8,128)}, u32[]{:S(2)}) %copy-start.1) | copy-done | bytes 262168
  2.8 0.0 copy-start.2
  2.8 0.9 %copy-done.2 = f32[512,128]{1,0:T(8,128)S(1)} copy-done((f32[512,128]{1,0:T(8,128)S(1)}, f32[512,128]{1,0:T(8,128)}, u32[]{:S(2)}) %copy-start.2) | copy-done | bytes 262168
  3.8 0.0 copy-start.3
  3.8 0.9 %copy-done.3 = f32[64,512]{1,0:T(8,128)S(1)} copy-done((f32[64,512]{1,0:T(8,128)S(1)}, f32[64,512]{1,0:T(8,128)}, u32[]{:S(2)}) %copy-start.3) | copy-done | bytes 131096
  4.7 0.0 copy-start.4
  4.7 0.9 %copy-done.4 = f32[64,512]{1,0:T(8,128)S(1)} copy-done((f32[64,512]{1,0:T(8,128)S(1)}, f32[64,512]{1,0:T(8,128)}, u32[]{:S(2)}) %copy-start.4) | copy-done | bytes 131096
  5.6 0.0 copy-start.5
  5.6 0.7 copy-done.5
  6.3 0.7 copy-done.6
  6.9 0.0 copy-start.7
  6.9 0.7 copy-done.7
  7.6 0.0 copy-start.8
  7.6 0.7 copy-done.8
  8.3 0.0 copy-start.9
  8.3 0.7 copy-done.9
  8.9 0.0 copy-start.10
  8.9 0.7 copy-done.10
  9.6 65.0 %shard_map.122 = (f32[512,128]{1,0:T(8,128)S(1)}, f32[512,128]{1,0:T(8,128)S(1)}) custom-call(f32[512,128]{1,0:T(8,128)S(1)} %copy-done.1, f32[1,512]{1,0:T(1,128)S(1)} %copy-done.6, f32[512,512]{1,0:T(8,128)S(1)} %copy-done, s32[8,8]{1,0:T(8,128)S(1)} %copy-done.5, s32[1,64]{1,0:T(1,128)S(1)} %copy-done.7, s32[1,64]{1,0:T(1,128)S(1)} %copy-done.8, ...), custom_call_target="tpu_custom_call" | custom-call | tf_op jit(solution)/shard_map/pallas_call | solution.py:336
  74.6 0.7 copy.15
  75.3 0.7 copy.16
  (1 shorter events, 0.0 us)
Async XLA Ops:
  0.6 1.2 %copy-start = (f32[512,512]{1,0:T(8,128)S(1)}, f32[512,512]{1,0:T(8,128)}, u32[]{:S(2)}) copy-start(f32[512,512]{1,0:T(8,128)} %values_ref.1) | copy-start | bytes 3145732
  1.9 0.9 %copy-start.1 = (f32[512,128]{1,0:T(8,128)S(1)}, f32[512,128]{1,0:T(8,128)}, u32[]{:S(2)}) copy-start(f32[512,128]{1,0:T(8,128)} %rs_ref.1) | copy-start | bytes 786436
  2.8 0.9 %copy-start.2 = (f32[512,128]{1,0:T(8,128)S(1)}, f32[512,128]{1,0:T(8,128)}, u32[]{:S(2)}) copy-start(f32[512,128]{1,0:T(8,128)} %factor_ref.1) | copy-start | bytes 786436
  3.8 0.9 %copy-start.3 = (f32[64,512]{1,0:T(8,128)S(1)}, f32[64,512]{1,0:T(8,128)}, u32[]{:S(2)}) copy-start(f32[64,512]{1,0:T(8,128)} %basis_ref.1) | copy-start | bytes 393220
  4.7 0.9 %copy-start.4 = (f32[64,512]{1,0:T(8,128)S(1)}, f32[64,512]{1,0:T(8,128)}, u32[]{:S(2)}) copy-start(f32[64,512]{1,0:T(8,128)} %coarse_ref.1) | copy-start | bytes 393220
  5.6 0.7 copy-start.5
  6.3 0.7 copy-start.6
  6.9 0.7 copy-start.7
  7.6 0.7 copy-start.8
  8.3 0.7 copy-start.9
  8.9 0.7 copy-start.10

commit v2 on v1

v2 whole, which is shorter than its diff:
```python
import functools

import jax
import jax.numpy as jnp
from jax import lax
from jax.experimental import pallas as pl
from jax.experimental.pallas import tpu as pltpu
from jax.sharding import PartitionSpec as P

HIGHEST = lax.Precision.HIGHEST
MESH = pl.DeviceIdType.MESH
LANES = 128
SUBLANES = 8


def mm(a, b):
    return jnp.dot(a, b, precision=HIGHEST, preferred_element_type=jnp.float32)


def stack_dots(rows):
    pad = SUBLANES - len(rows)
    return jnp.concatenate(rows + [jnp.zeros((pad, rows[0].shape[1]), jnp.float32)], axis=0)


def column_dot(a, b):
    return jnp.sum(a * b, axis=0, keepdims=True)


def split(x):
    high = x.astype(jnp.bfloat16)
    low = (x - high.astype(jnp.float32)).astype(jnp.bfloat16)
    return high, low


def keep(pair_ref, x, rows=slice(None)):
    high, low = split(x)
    pair_ref[0, rows] = high
    pair_ref[1, rows] = low


def mm3(pair_ref, b, rows=slice(None)):
    high, low = b
    n = high.shape[1]
    wide = jnp.dot(
        pair_ref[0, rows], jnp.concatenate([high, low], axis=1), preferred_element_type=jnp.float32
    )
    cross = jnp.dot(pair_ref[1, rows], high, preferred_element_type=jnp.float32)
    return wide[:, :n] + (wide[:, n:] + cross)


N_IN = 11


def kernel(n_group, n_sub, *refs):
    hbm = refs[:N_IN]
    x_ref, r_ref = refs[N_IN : N_IN + 2]
    held = refs[N_IN + 2 : 2 * N_IN + 2]
    (
        dense,
        dense_pair,
        near_pair,
        inv_diag,
        diag,
        basis_pair,
        basis_t_pair,
        select_pair,
        spread_pair,
        solve_pair,
        extend_out,
        extend_in,
        weight_out,
        weight_in,
        group_out,
        group_buf,
        sub_buf,
        face_out,
        face_in,
        group_dots,
        sub_dots,
        load_sem,
        send_sem,
        recv_sem,
        step_sem,
    ) = refs[2 * N_IN + 2 :]
    (
        rs_ref,
        mass_ref,
        values_ref,
        cols_ref,
        faces_ref,
        lands_ref,
        counts_ref,
        fweight_ref,
        factor_ref,
        basis_ref,
        coarse_ref,
    ) = held

    def load(i):
        return pltpu.make_async_copy(hbm[i], held[i], load_sem.at[i])

    for i in (9, 0, 4, 5, 6, 7, 10, 2, 3, 8, 1):
        load(i).start()

    me_g = lax.axis_index("group")
    me_s = lax.axis_index("sub")
    core = lax.rem(me_g, 2)
    sibling = me_g + 1 - 2 * core
    n_rows, n_rhs = rs_ref.shape
    n_slots = faces_ref.shape[1]
    per_peer = n_slots // n_sub
    n_blocks, n_stored = cols_ref.shape
    block_rows = n_rows // n_blocks
    n_coarse = basis_ref.shape[0]
    half = n_coarse // 2
    total_coarse = coarse_ref.shape[1]
    factor_rows = factor_ref.shape[1]
    n_factors = n_rows // factor_rows

    barrier = pltpu.get_barrier_semaphore()
    for step in range(1, n_group):
        peer = lax.rem(me_g + step, n_group)
        pl.semaphore_signal(barrier, inc=1, device_id=(peer, me_s), device_id_type=MESH)
    for step in range(1, n_sub):
        peer = lax.rem(me_s + step, n_sub)
        pl.semaphore_signal(barrier, inc=1, device_id=(me_g, peer), device_id_type=MESH)

    sent = []

    def send(src, dst, channel, arrived, peer):
        pltpu.make_async_remote_copy(
            src_ref=src,
            dst_ref=dst,
            send_sem=send_sem.at[channel],
            recv_sem=arrived,
            device_id=peer,
            device_id_type=MESH,
        ).start()

    def over_sub(channel, src_of, dst, arrived_of=None):
        for step in range(1, n_sub):
            peer = lax.rem(me_s + step, n_sub)
            arrived = recv_sem.at[channel] if arrived_of is None else arrived_of(step)
            send(src_of(peer), dst, channel, arrived, (me_g, peer))

    def over_group(channel, src_of, dst):
        for step in range(1, n_group):
            peer = lax.rem(me_g + step, n_group)
            send(src_of(peer), dst, channel, recv_sem.at[channel], (peer, me_s))

    def arrive(channel, part):
        pltpu.make_async_copy(part, part, recv_sem.at[channel]).wait()
        sent.append((channel, part))

    def send_coarse(phase, part, dots):
        group_out[phase, 0] = jnp.concatenate([part[:half], dots], axis=0)
        group_out[phase, 1] = jnp.concatenate([part[half:], dots], axis=0)
        group_buf[phase, me_g] = group_out[phase, core]
        if phase == 0:
            pl.semaphore_wait(barrier, n_group - 1 + n_sub - 1)
        over_group(
            2 + phase,
            lambda peer: group_out.at[phase, lax.rem(peer, 2)],
            group_buf.at[phase, me_g],
        )

    load(9).wait()
    load(0).wait()
    resid = rs_ref[...]
    send_coarse(0, mm(basis_ref[...], resid), jnp.zeros((SUBLANES, n_rhs), jnp.float32))

    for i in (4, 5, 6, 7):
        load(i).wait()
    slot = lax.broadcasted_iota(jnp.int32, (1, n_slots), 1)
    slot_peer = lax.broadcasted_iota(jnp.int32, (n_sub, n_slots), 1) // per_peer
    peer_ids = lax.broadcasted_iota(jnp.int32, (n_sub, n_slots), 0)
    of_peer = jnp.where(slot_peer == peer_ids, jnp.float32(1.0), jnp.float32(0.0))
    count_row = mm(
        jnp.broadcast_to(counts_ref[...].astype(jnp.float32), (SUBLANES, n_sub)), of_peer
    )[0:1]
    in_peer = (slot % per_peer).astype(jnp.float32)
    weights = jnp.where(in_peer < count_row - 0.5, fweight_ref[...], jnp.float32(0.0))
    row_ids = lax.broadcasted_iota(jnp.int32, (n_rows, n_slots), 0)
    face_hot = jnp.where(row_ids == faces_ref[...], weights, jnp.float32(0.0))
    land_hot = jnp.where(row_ids == lands_ref[...], jnp.float32(1.0), jnp.float32(0.0))
    spread = jnp.concatenate([land_hot, face_hot], axis=1)
    keep(spread_pair, spread)
    select = jnp.concatenate([face_hot, land_hot], axis=1).T
    keep(select_pair, select)

    weight_out[...] = mm(
        select[:n_slots, :], jnp.ones((n_rows, n_rhs), jnp.float32)
    ).reshape(n_sub, per_peer, n_rhs)
    weight_in[pl.ds(me_s, 1)] = weight_out[pl.ds(me_s, 1)]
    over_sub(0, lambda peer: weight_out.at[peer], weight_in.at[me_s])

    def gather_group(phase):
        arrive(2 + phase, group_buf.at[phase, pl.ds(0, n_group - 1)])
        total = group_buf[phase, 0]
        for g in range(1, n_group):
            total = total + group_buf[phase, g]
        sub_buf[phase, core, me_s] = total
        mine = sub_buf.at[phase, core, me_s]
        over_sub(6 + phase, lambda peer: mine, mine, lambda step: step_sem.at[phase, step])
        forward(phase, me_s)

    def forward(phase, slot_of):
        part = sub_buf.at[phase, core, slot_of, pl.ds(0, half)]
        send(part, part, 13 + phase, recv_sem.at[13 + phase], (sibling, me_s))

    gather_group(0)

    load(10).wait()
    basis_t = basis_ref[...].T
    keep(basis_t_pair, basis_t)
    keep(basis_pair, basis_ref[...])
    keep(solve_pair, coarse_ref[...], slice(0, n_coarse))
    reach = mm(mm(select, basis_t), coarse_ref[...])
    extend_out[:, :per_peer, :] = reach[:n_slots].reshape(n_sub, per_peer, total_coarse)
    extend_out[:, per_peer:, :] = reach[n_slots:].reshape(n_sub, per_peer, total_coarse)
    extend_in[pl.ds(me_s, 1)] = extend_out[pl.ds(me_s, 1)]
    over_sub(1, lambda peer: extend_out.at[peer], extend_in.at[me_s])

    load(2).wait()
    load(3).wait()
    n_tiles = n_rows // LANES
    stored = n_stored * block_rows
    stored_tiles = stored // LANES
    stored_ids = lax.broadcasted_iota(jnp.int32, (n_stored, stored), 0)
    lane_block = lax.broadcasted_iota(jnp.int32, (n_stored, stored), 1) // block_rows
    of_stored = jnp.where(stored_ids == lane_block, jnp.float32(1.0), jnp.float32(0.0))
    wide_cols = mm(cols_ref[...].astype(jnp.float32), of_stored)
    high = lax.broadcasted_iota(jnp.int32, (1, LANES), 1) // block_rows
    for b in range(n_blocks):
        rows = slice(b * block_rows, (b + 1) * block_rows)
        sums = [jnp.zeros((block_rows, LANES), jnp.float32) for _ in range(n_tiles)]
        for t in range(stored_tiles):
            tile = values_ref[rows, t * LANES : (t + 1) * LANES]
            turned = pltpu.roll(tile, block_rows, 1)
            straight_cols = wide_cols[b : b + 1, t * LANES : (t + 1) * LANES]
            turned_cols = pltpu.roll(straight_cols, block_rows, 1)
            for u in range(n_tiles):
                target = (2 * u + high).astype(jnp.float32)
                straight = jnp.abs(straight_cols - target) < 0.5
                swapped = jnp.abs(turned_cols - target) < 0.5
                sums[u] = (
                    sums[u]
                    + jnp.where(straight, tile, jnp.float32(0.0))
                    + jnp.where(swapped, turned, jnp.float32(0.0))
                )
        for u in range(n_tiles):
            dense[rows, u * LANES : (u + 1) * LANES] = sums[u]
    both = dense[...] + dense[...].T
    keep(dense_pair, both)
    degree = mm(both, jnp.ones((n_rows, n_rhs), jnp.float32))

    load(8).wait()
    for i in range(n_factors):
        rows = slice(i * factor_rows, (i + 1) * factor_rows)
        part = factor_ref[rows, :]
        keep(near_pair, mm(part.T, part), rows)

    load(1).wait()
    mass_col = jnp.broadcast_to(mass_ref[...], (n_rhs, n_rows)).T
    arrive(0, weight_in.at[pl.ds(0, n_sub - 1)])
    degree = degree + mm(
        spread,
        jnp.concatenate(
            [
                weight_in[...].reshape(n_slots, n_rhs),
                jnp.ones((n_slots, n_rhs), jnp.float32),
            ],
            axis=0,
        ),
    )
    diag[...] = mass_col + degree
    inv_diag[...] = 1.0 / diag[...]

    def send_local(phase, field, pair):
        parts = []
        for i in range(n_factors):
            rows = slice(i * factor_rows, (i + 1) * factor_rows)
            parts.append(mm3(near_pair, (pair[0][rows], pair[1][rows]), rows))
        local_part = field * inv_diag[...] + jnp.concatenate(parts, axis=0)
        picked = mm3(select_pair, split(local_part))
        face_out[phase, :, :per_peer, :] = picked[:n_slots].reshape(n_sub, per_peer, n_rhs)
        face_out[phase, :, per_peer:, :] = picked[n_slots:].reshape(n_sub, per_peer, n_rhs)
        face_in[phase, me_s] = face_out[phase, me_s]
        over_sub(10 + phase, lambda peer: face_out.at[phase, peer], face_in.at[phase, me_s])
        return local_part

    def receive(phase, local_part):
        for step in range(1, n_sub):
            origin = lax.rem(me_s + n_sub - step, n_sub)
            part = sub_buf.at[phase, core, origin]
            pltpu.make_async_copy(part, part, step_sem.at[phase, step]).wait()
            forward(phase, origin)
        dots = jnp.sum(sub_buf[phase, core, :, half:, :], axis=0)
        if phase == 0:
            arrive(1, extend_in.at[pl.ds(0, n_sub - 1)])
            keep(
                solve_pair,
                extend_in[...].reshape(2 * n_slots, total_coarse),
                slice(n_coarse, n_coarse + 2 * n_slots),
            )
        sent.append((6 + phase, sub_buf.at[phase, 0, pl.ds(0, n_sub - 1)]))
        arrive(13 + phase, sub_buf.at[phase, 0, :, pl.ds(0, half)])
        whole = jnp.concatenate(
            [sub_buf[phase, 0, :, :half, :], sub_buf[phase, 1, :, :half, :]], axis=1
        ).reshape(total_coarse, n_rhs)
        solved = mm3(solve_pair, split(whole))
        field = local_part + mm3(basis_t_pair, split(solved[:n_coarse]))
        arrive(10 + phase, face_in.at[phase, pl.ds(0, n_sub - 1)])
        far = solved[n_coarse:].reshape(n_sub, 2 * per_peer, n_rhs) + face_in[phase]
        far = jnp.concatenate(
            [
                far[:, :per_peer, :].reshape(n_slots, n_rhs),
                far[:, per_peer:, :].reshape(n_slots, n_rhs),
            ],
            axis=0,
        )
        return field, far, dots

    def operate(field, far):
        pair = split(field)
        held_field = pair[0].astype(jnp.float32) + pair[1].astype(jnp.float32)
        return diag[...] * held_field - mm3(dense_pair, pair) - mm3(spread_pair, split(far))

    local_part = send_local(0, resid, split(resid))
    z, z_far, _ = receive(0, local_part)
    image = operate(z, z_far)
    pair = split(image)
    send_coarse(
        1, mm3(basis_pair, pair), stack_dots([column_dot(resid, z), column_dot(z, image)])
    )
    local_part = send_local(1, image, pair)
    gather_group(1)
    m_image, m_far, dots = receive(1, local_part)
    gamma, bent = dots[0:1], dots[1:2]
    alpha = gamma / bent
    direction = z
    answer = alpha * direction
    resid = resid - alpha * image
    z = z - alpha * m_image
    z_far = z_far - alpha * m_far
    z_image = operate(z, z_far)
    pair = split(z_image)
    send_coarse(
        2,
        mm3(basis_pair, pair),
        stack_dots([column_dot(resid, z), column_dot(z, z_image), column_dot(z, image)]),
    )
    local_part = send_local(2, z_image, pair)
    gather_group(2)
    m_z_image, m_z_far, dots = receive(2, local_part)
    beta = dots[0:1] / gamma
    gamma = dots[0:1]
    bent = dots[1:2] + beta * (2.0 * dots[2:3] + beta * bent)
    alpha = gamma / bent
    direction = z + beta * direction
    image = z_image + beta * image
    answer = answer + alpha * direction
    resid = resid - alpha * image
    z = z - alpha * (m_z_image + beta * m_image)
    z_far = z_far - alpha * (m_z_far + beta * m_far)
    z_image = operate(z, z_far)
    group_dots[me_g] = stack_dots(
        [column_dot(resid, z), column_dot(z, z_image), column_dot(z, image)]
    )
    over_group(5, lambda peer: group_dots.at[me_g], group_dots.at[me_g])
    arrive(5, group_dots.at[pl.ds(0, n_group - 1)])
    sub_dots[me_s] = jnp.sum(group_dots[...], axis=0)
    over_sub(9, lambda peer: sub_dots.at[me_s], sub_dots.at[me_s])
    arrive(9, sub_dots.at[pl.ds(0, n_sub - 1)])
    dots = jnp.sum(sub_dots[...], axis=0)
    beta = dots[0:1] / gamma
    gamma = dots[0:1]
    bent = dots[1:2] + beta * (2.0 * dots[2:3] + beta * bent)
    alpha = gamma / bent
    x_ref[...] = answer + alpha * (z + beta * direction)
    r_ref[...] = resid - alpha * (z_image + beta * image)

    for channel, part in sent:
        pltpu.make_async_copy(part, part, send_sem.at[channel]).wait()


def local(n_group, n_sub, *args):
    right_side, face_rows = args[0], args[4]
    basis, coarse_inverse = args[9], args[10]
    n_rows, n_rhs = right_side.shape
    n_slots = face_rows.shape[1]
    per_peer = n_slots // n_sub
    n_coarse = basis.shape[0]
    total_coarse = coarse_inverse.shape[1]
    factor_rows = args[8].shape[1]
    f32 = jnp.float32
    bf16 = jnp.bfloat16
    vmem = pl.BlockSpec(memory_space=pltpu.VMEM)
    message = n_coarse // 2 + SUBLANES
    scratch = [pltpu.VMEM(arg.shape, arg.dtype) for arg in args]
    scratch += [
        pltpu.VMEM((n_rows, n_rows), f32),
        pltpu.VMEM((2, n_rows, n_rows), bf16),
        pltpu.VMEM((2, n_rows, factor_rows), bf16),
        pltpu.VMEM((n_rows, n_rhs), f32),
        pltpu.VMEM((n_rows, n_rhs), f32),
        pltpu.VMEM((2, n_coarse, n_rows), bf16),
        pltpu.VMEM((2, n_rows, n_coarse), bf16),
        pltpu.VMEM((2, 2 * n_slots, n_rows), bf16),
        pltpu.VMEM((2, n_rows, 2 * n_slots), bf16),
        pltpu.VMEM((2, n_coarse + 2 * n_slots, total_coarse), bf16),
        pltpu.VMEM((n_sub, 2 * per_peer, total_coarse), f32),
        pltpu.VMEM((n_sub, 2 * per_peer, total_coarse), f32),
        pltpu.VMEM((n_sub, per_peer, n_rhs), f32),
        pltpu.VMEM((n_sub, per_peer, n_rhs), f32),
        pltpu.VMEM((3, 2, message, n_rhs), f32),
        pltpu.VMEM((3, n_group, message, n_rhs), f32),
        pltpu.VMEM((3, 2, n_sub, message, n_rhs), f32),
        pltpu.VMEM((3, n_sub, 2 * per_peer, n_rhs), f32),
        pltpu.VMEM((3, n_sub, 2 * per_peer, n_rhs), f32),
        pltpu.VMEM((n_group, SUBLANES, n_rhs), f32),
        pltpu.VMEM((n_sub, SUBLANES, n_rhs), f32),
        pltpu.SemaphoreType.DMA((N_IN,)),
        pltpu.SemaphoreType.DMA((16,)),
        pltpu.SemaphoreType.DMA((16,)),
        pltpu.SemaphoreType.DMA((3, n_sub)),
    ]
    field = jax.ShapeDtypeStruct((n_rows, n_rhs), f32)
    return pl.pallas_call(
        functools.partial(kernel, n_group, n_sub),
        out_shape=(field, field),
        in_specs=[pl.BlockSpec(memory_space=pl.ANY)] * N_IN,
        out_specs=(vmem, vmem),
        scratch_shapes=scratch,
        compiler_params=pltpu.CompilerParams(
            collective_id=0, has_side_effects=True, vmem_limit_bytes=56 * 1024 * 1024
        ),
    )(*args)


def solution(mesh):
    n_group, n_sub = mesh.shape["group"], mesh.shape["sub"]
    rows = P(("group", "sub"), None)
    return jax.shard_map(
        functools.partial(local, n_group, n_sub),
        mesh=mesh,
        in_specs=(rows,) * 10 + (P("sub", None),),
        out_specs=(rows, rows),
        check_vma=False,
    )
```

time: 76.4 us -> 55.1 us (0.72)
  Pallas kernels: 65 us -> 51.9 us
  local copies, waits for them, and re-layouts: 10.3 us -> 2.42 us
    pallas_call x1, Pallas kernels: 65 us -> 51.9 us  [local(): pl.pallas_call(functools.partial(kernel, n_group, n_sub), out_shape=(fiel...]
    unnamed x24 -> x4, local copies, waits for them, and re-layouts: 10.3 us -> 2.42 us
where the time goes in v2:
time: 55.1 us; the launch traced here: 54.9 us
  Pallas kernels  51.9 us (94%)
  local copies, waits for them, and re-layouts  2.42 us (4%)
  between operations  0.65 us (1%)
    pallas_call x1, Pallas kernels, local(): pl.pallas_call(functools.partial(kernel, n_group, n_sub), out_shape=(fiel...  51.9 us
    unnamed x4, local copies, waits for them, and re-layouts  2.42 us

profile of v2, /device:TPU:0, one launch (start us, length us, event | category | flops | bytes accessed | tf_op | source)
XLA Modules:
  0.0 54.9 jit_solution(10126081093718508016)
XLA Ops:
  0.6 51.9 %shard_map.122 = (f32[512,128]{1,0:T(8,128)}, f32[512,128]{1,0:T(8,128)}) custom-call(f32[512,128]{1,0:T(8,128)} %refs_0_.1, f32[1,512]{1,0:T(1,128)} %refs_1_.1, f32[512,512]{1,0:T(8,128)} %refs_2_.1, s32[8,8]{1,0:T(8,128)} %refs_3_.1, s32[1,64]{1,0:T(1,128)} %refs_4_.1, s32[1,64]{1,0:T(1,128)} %refs_5_.1, s32[1,8]{1,0:T(1,128)} %refs_6_.1, ...), custom_call_target="tpu_custom_call" | custom-call | tf_op jit(solution)/shard_map/pallas_call | solution.py:429
  52.5 0.0 copy-start
  52.5 1.7 %copy.15 = f32[512,128]{1,0:T(8,128)} copy(f32[512,128]{1,0:T(8,128)} %get-tuple-element.4) | data formatting | bytes 524288
  54.2 0.0 copy-done
  54.2 0.7 %copy.16 = f32[512,128]{1,0:T(8,128)} copy(f32[512,128]{1,0:T(8,128)S(1)} %copy-done) | data formatting | bytes 524288
Async XLA Ops:
  52.5 1.7 %copy-start = (f32[512,128]{1,0:T(8,128)S(1)}, f32[512,128]{1,0:T(8,128)}, u32[]{:S(2)}) copy-start(f32[512,128]{1,0:T(8,128)} %get-tuple-element.5) | copy-start | bytes 786436

commit v3 on v2

--- a/solution.py
+++ b/solution.py
@@ -53,8 +53,8 @@
 
 def kernel(n_group, n_sub, *refs):
     hbm = refs[:N_IN]
-    x_ref, r_ref = refs[N_IN : N_IN + 2]
-    held = refs[N_IN + 2 : 2 * N_IN + 2]
+    out_ref = refs[N_IN]
+    held = refs[N_IN + 1 : 2 * N_IN + 1]
     (
         dense,
         dense_pair,
@@ -81,7 +81,7 @@
         send_sem,
         recv_sem,
         step_sem,
-    ) = refs[2 * N_IN + 2 :]
+    ) = refs[2 * N_IN + 1 :]
     (
         rs_ref,
         mass_ref,
@@ -152,6 +152,9 @@
         pltpu.make_async_copy(part, part, recv_sem.at[channel]).wait()
         sent.append((channel, part))
 
+    def message(phase):
+        return pl.ds(0, half if phase == 0 else half + SUBLANES)
+
     def send_coarse(phase, part, dots):
         group_out[phase, 0] = jnp.concatenate([part[:half], dots], axis=0)
         group_out[phase, 1] = jnp.concatenate([part[half:], dots], axis=0)
@@ -160,8 +163,8 @@
             pl.semaphore_wait(barrier, n_group - 1 + n_sub - 1)
         over_group(
             2 + phase,
-            lambda peer: group_out.at[phase, lax.rem(peer, 2)],
-            group_buf.at[phase, me_g],
+            lambda peer: group_out.at[phase, lax.rem(peer, 2), message(phase)],
+            group_buf.at[phase, me_g, message(phase)],
         )
 
     load(9).wait()
@@ -195,12 +198,12 @@
     over_sub(0, lambda peer: weight_out.at[peer], weight_in.at[me_s])
 
     def gather_group(phase):
-        arrive(2 + phase, group_buf.at[phase, pl.ds(0, n_group - 1)])
-        total = group_buf[phase, 0]
+        arrive(2 + phase, group_buf.at[phase, pl.ds(0, n_group - 1), message(phase)])
+        total = group_buf[phase, 0, message(phase)]
         for g in range(1, n_group):
-            total = total + group_buf[phase, g]
-        sub_buf[phase, core, me_s] = total
-        mine = sub_buf.at[phase, core, me_s]
+            total = total + group_buf[phase, g, message(phase)]
+        sub_buf[phase, core, me_s, message(phase)] = total
+        mine = sub_buf.at[phase, core, me_s, message(phase)]
         over_sub(6 + phase, lambda peer: mine, mine, lambda step: step_sem.at[phase, step])
         forward(phase, me_s)
 
@@ -215,11 +218,11 @@
     keep(basis_t_pair, basis_t)
     keep(basis_pair, basis_ref[...])
     keep(solve_pair, coarse_ref[...], slice(0, n_coarse))
-    reach = mm(mm(select, basis_t), coarse_ref[...])
-    extend_out[:, :per_peer, :] = reach[:n_slots].reshape(n_sub, per_peer, total_coarse)
-    extend_out[:, per_peer:, :] = reach[n_slots:].reshape(n_sub, per_peer, total_coarse)
-    extend_in[pl.ds(me_s, 1)] = extend_out[pl.ds(me_s, 1)]
-    over_sub(1, lambda peer: extend_out.at[peer], extend_in.at[me_s])
+    load(8).wait()
+    for i in range(n_factors):
+        rows = slice(i * factor_rows, (i + 1) * factor_rows)
+        part = factor_ref[rows, :]
+        keep(near_pair, mm(part.T, part), rows)
 
     load(2).wait()
     load(3).wait()
@@ -231,6 +234,113 @@
     of_stored = jnp.where(stored_ids == lane_block, jnp.float32(1.0), jnp.float32(0.0))
     wide_cols = mm(cols_ref[...].astype(jnp.float32), of_stored)
     high = lax.broadcasted_iota(jnp.int32, (1, LANES), 1) // block_rows
+    row_sums = mm(values_ref[...], jnp.ones((n_stored * block_rows, n_rhs), jnp.float32))
+    col_parts = jnp.concatenate(
+        [
+            jnp.sum(values_ref[b * block_rows : (b + 1) * block_rows, :], axis=0, keepdims=True)
+            for b in range(n_blocks)
+        ],
+        axis=0,
+    )
+    col_sums = [jnp.zeros((n_blocks, LANES), jnp.float32) for _ in range(n_tiles)]
+    for t in range(stored_tiles):
+        tile = col_parts[:, t * LANES : (t + 1) * LANES]
+        turned = pltpu.roll(tile, block_rows, 1)
+        straight_cols = wide_cols[:, t * LANES : (t + 1) * LANES]
+        turned_cols = pltpu.roll(straight_cols, block_rows, 1)
+        for u in range(n_tiles):
+            target = (2 * u + high).astype(jnp.float32)
+            col_sums[u] = (
+                col_sums[u]
+                + jnp.where(jnp.abs(straight_cols - target) < 0.5, tile, jnp.float32(0.0))
+                + jnp.where(jnp.abs(turned_cols - target) < 0.5, turned, jnp.float32(0.0))
+            )
+    col_row = jnp.concatenate(
+        [jnp.sum(part, axis=0, keepdims=True) for part in col_sums], axis=1
+    )
+    load(1).wait()
+    mass_col = jnp.broadcast_to(mass_ref[...] + col_row, (n_rhs, n_rows)).T
+    arrive(0, weight_in.at[pl.ds(0, n_sub - 1)])
+    degree = row_sums + mm(
+        spread,
+        jnp.concatenate(
+            [
+                weight_in[...].reshape(n_slots, n_rhs),
+                jnp.ones((n_slots, n_rhs), jnp.float32),
+            ],
+            axis=0,
+        ),
+    )
+    diag[...] = mass_col + degree
+    inv_diag[...] = 1.0 / diag[...]
+
+    def local_of(field, pair):
+        parts = []
+        for i in range(n_factors):
+            rows = slice(i * factor_rows, (i + 1) * factor_rows)
+            parts.append(mm3(near_pair, (pair[0][rows], pair[1][rows]), rows))
+        return field * inv_diag[...] + jnp.concatenate(parts, axis=0)
+
+    def send_faces(phase, field):
+        picked = mm3(select_pair, split(field))
+        face_out[phase, :, :per_peer, :] = picked[:n_slots].reshape(n_sub, per_peer, n_rhs)
+        face_out[phase, :, per_peer:, :] = picked[n_slots:].reshape(n_sub, per_peer, n_rhs)
+        face_in[phase, me_s] = face_out[phase, me_s]
+        over_sub(10 + phase, lambda peer: face_out.at[phase, peer], face_in.at[phase, me_s])
+
+    def receive(phase, local_part):
+        for step in range(1, n_sub):
+            origin = lax.rem(me_s + n_sub - step, n_sub)
+            part = sub_buf.at[phase, core, origin, message(phase)]
+            pltpu.make_async_copy(part, part, step_sem.at[phase, step]).wait()
+            forward(phase, origin)
+        dots = None if phase == 0 else jnp.sum(sub_buf[phase, core, :, half:, :], axis=0)
+        if phase == 1:
+            arrive(1, extend_in.at[pl.ds(0, n_sub - 1)])
+            keep(
+                solve_pair,
+                extend_in[...].reshape(2 * n_slots, total_coarse),
+                slice(n_coarse, n_coarse + 2 * n_slots),
+            )
+        sent.append((6 + phase, sub_buf.at[phase, 0, pl.ds(0, n_sub - 1), message(phase)]))
+        arrive(13 + phase, sub_buf.at[phase, 0, :, pl.ds(0, half)])
+        whole = jnp.concatenate(
+            [sub_buf[phase, 0, :, :half, :], sub_buf[phase, 1, :, :half, :]], axis=1
+        ).reshape(total_coarse, n_rhs)
+        pair = split(whole)
+        if phase == 0:
+            solved = mm3(solve_pair, pair, slice(0, n_coarse))
+            return local_part + mm3(basis_t_pair, split(solved)), None, None
+        solved = mm3(solve_pair, pair)
+        field = local_part + mm3(basis_t_pair, split(solved[:n_coarse]))
+        return field, receive_faces(phase, solved[n_coarse:]), dots
+
+    def receive_faces(phase, solved):
+        arrive(10 + phase, face_in.at[phase, pl.ds(0, n_sub - 1)])
+        far = face_in[phase]
+        if solved is not None:
+            far = far + solved.reshape(n_sub, 2 * per_peer, n_rhs)
+        return jnp.concatenate(
+            [
+                far[:, :per_peer, :].reshape(n_slots, n_rhs),
+                far[:, per_peer:, :].reshape(n_slots, n_rhs),
+            ],
+            axis=0,
+        )
+
+    def operate(field, far):
+        pair = split(field)
+        held_field = pair[0].astype(jnp.float32) + pair[1].astype(jnp.float32)
+        return diag[...] * held_field - mm3(dense_pair, pair) - mm3(spread_pair, split(far))
+
+    z, _, _ = receive(0, local_of(resid, split(resid)))
+    send_faces(0, z)
+    reach = mm(mm(select, basis_t), coarse_ref[...])
+    extend_out[:, :per_peer, :] = reach[:n_slots].reshape(n_sub, per_peer, total_coarse)
+    extend_out[:, per_peer:, :] = reach[n_slots:].reshape(n_sub, per_peer, total_coarse)
+    extend_in[pl.ds(me_s, 1)] = extend_out[pl.ds(me_s, 1)]
+    over_sub(1, lambda peer: extend_out.at[peer], extend_in.at[me_s])
+
     for b in range(n_blocks):
         rows = slice(b * block_rows, (b + 1) * block_rows)
         sums = [jnp.zeros((block_rows, LANES), jnp.float32) for _ in range(n_tiles)]
@@ -250,90 +360,15 @@
                 )
         for u in range(n_tiles):
             dense[rows, u * LANES : (u + 1) * LANES] = sums[u]
-    both = dense[...] + dense[...].T
-    keep(dense_pair, both)
-    degree = mm(both, jnp.ones((n_rows, n_rhs), jnp.float32))
-
-    load(8).wait()
-    for i in range(n_factors):
-        rows = slice(i * factor_rows, (i + 1) * factor_rows)
-        part = factor_ref[rows, :]
-        keep(near_pair, mm(part.T, part), rows)
-
-    load(1).wait()
-    mass_col = jnp.broadcast_to(mass_ref[...], (n_rhs, n_rows)).T
-    arrive(0, weight_in.at[pl.ds(0, n_sub - 1)])
-    degree = degree + mm(
-        spread,
-        jnp.concatenate(
-            [
-                weight_in[...].reshape(n_slots, n_rhs),
-                jnp.ones((n_slots, n_rhs), jnp.float32),
-            ],
-            axis=0,
-        ),
-    )
-    diag[...] = mass_col + degree
-    inv_diag[...] = 1.0 / diag[...]
-
-    def send_local(phase, field, pair):
-        parts = []
-        for i in range(n_factors):
-            rows = slice(i * factor_rows, (i + 1) * factor_rows)
-            parts.append(mm3(near_pair, (pair[0][rows], pair[1][rows]), rows))
-        local_part = field * inv_diag[...] + jnp.concatenate(parts, axis=0)
-        picked = mm3(select_pair, split(local_part))
-        face_out[phase, :, :per_peer, :] = picked[:n_slots].reshape(n_sub, per_peer, n_rhs)
-        face_out[phase, :, per_peer:, :] = picked[n_slots:].reshape(n_sub, per_peer, n_rhs)
-        face_in[phase, me_s] = face_out[phase, me_s]
-        over_sub(10 + phase, lambda peer: face_out.at[phase, peer], face_in.at[phase, me_s])
-        return local_part
-
-    def receive(phase, local_part):
-        for step in range(1, n_sub):
-            origin = lax.rem(me_s + n_sub - step, n_sub)
-            part = sub_buf.at[phase, core, origin]
-            pltpu.make_async_copy(part, part, step_sem.at[phase, step]).wait()
-            forward(phase, origin)
-        dots = jnp.sum(sub_buf[phase, core, :, half:, :], axis=0)
-        if phase == 0:
-            arrive(1, extend_in.at[pl.ds(0, n_sub - 1)])
-            keep(
-                solve_pair,
-                extend_in[...].reshape(2 * n_slots, total_coarse),
-                slice(n_coarse, n_coarse + 2 * n_slots),
-            )
-        sent.append((6 + phase, sub_buf.at[phase, 0, pl.ds(0, n_sub - 1)]))
-        arrive(13 + phase, sub_buf.at[phase, 0, :, pl.ds(0, half)])
-        whole = jnp.concatenate(
-            [sub_buf[phase, 0, :, :half, :], sub_buf[phase, 1, :, :half, :]], axis=1
-        ).reshape(total_coarse, n_rhs)
-        solved = mm3(solve_pair, split(whole))
-        field = local_part + mm3(basis_t_pair, split(solved[:n_coarse]))
-        arrive(10 + phase, face_in.at[phase, pl.ds(0, n_sub - 1)])
-        far = solved[n_coarse:].reshape(n_sub, 2 * per_peer, n_rhs) + face_in[phase]
-        far = jnp.concatenate(
-            [
-                far[:, :per_peer, :].reshape(n_slots, n_rhs),
-                far[:, per_peer:, :].reshape(n_slots, n_rhs),
-            ],
-            axis=0,
-        )
-        return field, far, dots
-
-    def operate(field, far):
-        pair = split(field)
-        held_field = pair[0].astype(jnp.float32) + pair[1].astype(jnp.float32)
-        return diag[...] * held_field - mm3(dense_pair, pair) - mm3(spread_pair, split(far))
-
-    local_part = send_local(0, resid, split(resid))
-    z, z_far, _ = receive(0, local_part)
+    keep(dense_pair, dense[...] + dense[...].T)
+    z_far = receive_faces(0, None)
     image = operate(z, z_far)
     pair = split(image)
     send_coarse(
         1, mm3(basis_pair, pair), stack_dots([column_dot(resid, z), column_dot(z, image)])
     )
-    local_part = send_local(1, image, pair)
+    local_part = local_of(image, pair)
+    send_faces(1, local_part)
     gather_group(1)
     m_image, m_far, dots = receive(1, local_part)
     gamma, bent = dots[0:1], dots[1:2]
@@ -350,7 +385,8 @@
         mm3(basis_pair, pair),
         stack_dots([column_dot(resid, z), column_dot(z, z_image), column_dot(z, image)]),
     )
-    local_part = send_local(2, z_image, pair)
+    local_part = local_of(z_image, pair)
+    send_faces(2, local_part)
     gather_group(2)
     m_z_image, m_z_far, dots = receive(2, local_part)
     beta = dots[0:1] / gamma
@@ -377,8 +413,8 @@
     gamma = dots[0:1]
     bent = dots[1:2] + beta * (2.0 * dots[2:3] + beta * bent)
     alpha = gamma / bent
-    x_ref[...] = answer + alpha * (z + beta * direction)
-    r_ref[...] = resid - alpha * (z_image + beta * image)
+    out_ref[0] = answer + alpha * (z + beta * direction)
+    out_ref[1] = resid - alpha * (z_image + beta * image)
 
     for channel, part in sent:
         pltpu.make_async_copy(part, part, send_sem.at[channel]).wait()
@@ -425,17 +461,18 @@
         pltpu.SemaphoreType.DMA((16,)),
         pltpu.SemaphoreType.DMA((3, n_sub)),
     ]
-    field = jax.ShapeDtypeStruct((n_rows, n_rhs), f32)
-    return pl.pallas_call(
+    field = jax.ShapeDtypeStruct((2, n_rows, n_rhs), f32)
+    both = pl.pallas_call(
         functools.partial(kernel, n_group, n_sub),
-        out_shape=(field, field),
+        out_shape=field,
         in_specs=[pl.BlockSpec(memory_space=pl.ANY)] * N_IN,
-        out_specs=(vmem, vmem),
+        out_specs=vmem,
         scratch_shapes=scratch,
         compiler_params=pltpu.CompilerParams(
             collective_id=0, has_side_effects=True, vmem_limit_bytes=56 * 1024 * 1024
         ),
     )(*args)
+    return both[0], both[1]
 
 
 def solution(mesh):

time: 55.1 us -> 53.3 us (0.967)
  Pallas kernels: 51.9 us -> 50.6 us
  local copies, waits for them, and re-layouts: 2.42 us -> 1.85 us
    unnamed x4 -> x0, local copies, waits for them, and re-layouts: 2.42 us -> none
    squeeze x0 -> x1, local copies, waits for them, and re-layouts: none -> 1.85 us  [local(): return (both[0], both[1])]
    pallas_call x1, Pallas kernels: 51.9 us -> 50.6 us  [local(): pl.pallas_call(functools.partial(kernel, n_group, n_sub), out_shape=field...]
where the time goes in v3:
time: 53.3 us; the launch traced here: 53.1 us
  Pallas kernels  50.6 us (95%)
  local copies, waits for them, and re-layouts  1.85 us (3%)
  between operations  0.64 us (1%)
    pallas_call x1, Pallas kernels, local(): pl.pallas_call(functools.partial(kernel, n_group, n_sub), out_shape=field...  50.6 us
    squeeze x1, local copies, waits for them, and re-layouts, local(): return (both[0], both[1])  1.85 us

profile of v3, /device:TPU:0, one launch (start us, length us, event | category | flops | bytes accessed | tf_op | source)
XLA Modules:
  0.0 53.1 jit_solution(17296200668527980532)
XLA Ops:
  0.6 50.6 %shard_map.122 = f32[2,512,128]{2,1,0:T(8,128)} custom-call(f32[512,128]{1,0:T(8,128)} %refs_0_.1, f32[1,512]{1,0:T(1,128)} %refs_1_.1, f32[512,512]{1,0:T(8,128)} %refs_2_.1, s32[8,8]{1,0:T(8,128)} %refs_3_.1, s32[1,64]{1,0:T(1,128)} %refs_4_.1, s32[1,64]{1,0:T(1,128)} %refs_5_.1, s32[1,8]{1,0:T(1,128)} %refs_6_.1, f32[1,64]{1,0:T(1,128)} %refs_7_.1, ...), custom_call_target="tpu_custom_call" | custom-call | tf_op jit(solution)/shard_map/pallas_call | solution.py:465
  51.3 1.9 %slice_bitcast_fusion = (f32[512,128]{1,0:T(8,128)}, f32[512,128]{1,0:T(8,128)}) fusion(f32[2,512,128]{2,1,0:T(8,128)} %shard_map.122), kind=kLoop, calls=%fused_computation | loop fusion | bytes 1048576 | tf_op jit(solution)/shard_map/squeeze | solution.py:475

commit v4 on v3

--- a/solution.py
+++ b/solution.py
@@ -11,6 +11,7 @@
 MESH = pl.DeviceIdType.MESH
 LANES = 128
 SUBLANES = 8
+DOTS = 4
 
 
 def mm(a, b):
@@ -153,7 +154,7 @@
         sent.append((channel, part))
 
     def message(phase):
-        return pl.ds(0, half if phase == 0 else half + SUBLANES)
+        return pl.ds(0, half if phase == 0 else half + DOTS)
 
     def send_coarse(phase, part, dots):
         group_out[phase, 0] = jnp.concatenate([part[:half], dots], axis=0)
@@ -211,13 +212,26 @@
         part = sub_buf.at[phase, core, slot_of, pl.ds(0, half)]
         send(part, part, 13 + phase, recv_sem.at[13 + phase], (sibling, me_s))
 
+    def keep_solve(rows_of, rows):
+        for part in range(2):
+            columns = slice(part * (total_coarse // 2), (part + 1) * (total_coarse // 2))
+            keep(solve_pair.at[part], rows_of[:, columns], rows)
+
     gather_group(0)
 
     load(10).wait()
     basis_t = basis_ref[...].T
     keep(basis_t_pair, basis_t)
     keep(basis_pair, basis_ref[...])
-    keep(solve_pair, coarse_ref[...], slice(0, n_coarse))
+    by_row = coarse_ref[...].T.reshape(n_sub, n_coarse, n_coarse)
+    coarse = jnp.concatenate(
+        [
+            by_row[:, :half].reshape(total_coarse // 2, n_coarse),
+            by_row[:, half:].reshape(total_coarse // 2, n_coarse),
+        ],
+        axis=0,
+    ).T
+    keep_solve(coarse, slice(0, n_coarse))
     load(8).wait()
     for i in range(n_factors):
         rows = slice(i * factor_rows, (i + 1) * factor_rows)
@@ -289,29 +303,30 @@
         over_sub(10 + phase, lambda peer: face_out.at[phase, peer], face_in.at[phase, me_s])
 
     def receive(phase, local_part):
+        if phase == 1:
+            arrive(1, extend_in.at[pl.ds(0, n_sub - 1)])
+            keep_solve(
+                extend_in[...].reshape(2 * n_slots, total_coarse),
+                slice(n_coarse, n_coarse + 2 * n_slots),
+            )
         for step in range(1, n_sub):
             origin = lax.rem(me_s + n_sub - step, n_sub)
             part = sub_buf.at[phase, core, origin, message(phase)]
             pltpu.make_async_copy(part, part, step_sem.at[phase, step]).wait()
             forward(phase, origin)
-        dots = None if phase == 0 else jnp.sum(sub_buf[phase, core, :, half:, :], axis=0)
-        if phase == 1:
-            arrive(1, extend_in.at[pl.ds(0, n_sub - 1)])
-            keep(
-                solve_pair,
-                extend_in[...].reshape(2 * n_slots, total_coarse),
-                slice(n_coarse, n_coarse + 2 * n_slots),
-            )
+        dots = None if phase == 0 else jnp.sum(sub_buf[phase, core, :, half : half + DOTS, :], axis=0)
         sent.append((6 + phase, sub_buf.at[phase, 0, pl.ds(0, n_sub - 1), message(phase)]))
+        rows = slice(0, n_coarse if phase == 0 else n_coarse + 2 * n_slots)
+
+        def solve_half(part):
+            gathered = sub_buf[phase, part, :, :half, :].reshape(total_coarse // 2, n_rhs)
+            return mm3(solve_pair.at[part], split(gathered), rows)
+
+        solved = solve_half(core)
         arrive(13 + phase, sub_buf.at[phase, 0, :, pl.ds(0, half)])
-        whole = jnp.concatenate(
-            [sub_buf[phase, 0, :, :half, :], sub_buf[phase, 1, :, :half, :]], axis=1
-        ).reshape(total_coarse, n_rhs)
-        pair = split(whole)
+        solved = solved + solve_half(1 - core)
         if phase == 0:
-            solved = mm3(solve_pair, pair, slice(0, n_coarse))
             return local_part + mm3(basis_t_pair, split(solved)), None, None
-        solved = mm3(solve_pair, pair)
         field = local_part + mm3(basis_t_pair, split(solved[:n_coarse]))
         return field, receive_faces(phase, solved[n_coarse:]), dots
 
@@ -335,7 +350,7 @@
 
     z, _, _ = receive(0, local_of(resid, split(resid)))
     send_faces(0, z)
-    reach = mm(mm(select, basis_t), coarse_ref[...])
+    reach = mm(mm(select, basis_t), coarse)
     extend_out[:, :per_peer, :] = reach[:n_slots].reshape(n_sub, per_peer, total_coarse)
     extend_out[:, per_peer:, :] = reach[n_slots:].reshape(n_sub, per_peer, total_coarse)
     extend_in[pl.ds(me_s, 1)] = extend_out[pl.ds(me_s, 1)]
@@ -374,7 +389,7 @@
     gamma, bent = dots[0:1], dots[1:2]
     alpha = gamma / bent
     direction = z
-    answer = alpha * direction
+    first_alpha = alpha
     resid = resid - alpha * image
     z = z - alpha * m_image
     z_far = z_far - alpha * m_far
@@ -388,22 +403,24 @@
     local_part = local_of(z_image, pair)
     send_faces(2, local_part)
     gather_group(2)
+    answer = first_alpha * direction
     m_z_image, m_z_far, dots = receive(2, local_part)
     beta = dots[0:1] / gamma
     gamma = dots[0:1]
     bent = dots[1:2] + beta * (2.0 * dots[2:3] + beta * bent)
     alpha = gamma / bent
-    direction = z + beta * direction
+    last_z, last_beta, last_alpha = z, beta, alpha
+    z_far = z_far - alpha * (m_z_far + beta * m_far)
+    z = z - alpha * (m_z_image + beta * m_image)
     image = z_image + beta * image
-    answer = answer + alpha * direction
     resid = resid - alpha * image
-    z = z - alpha * (m_z_image + beta * m_image)
-    z_far = z_far - alpha * (m_z_far + beta * m_far)
     z_image = operate(z, z_far)
     group_dots[me_g] = stack_dots(
         [column_dot(resid, z), column_dot(z, z_image), column_dot(z, image)]
     )
     over_group(5, lambda peer: group_dots.at[me_g], group_dots.at[me_g])
+    direction = last_z + last_beta * direction
+    answer = answer + last_alpha * direction
     arrive(5, group_dots.at[pl.ds(0, n_group - 1)])
     sub_dots[me_s] = jnp.sum(group_dots[...], axis=0)
     over_sub(9, lambda peer: sub_dots.at[me_s], sub_dots.at[me_s])
@@ -444,7 +461,7 @@
         pltpu.VMEM((2, n_rows, n_coarse), bf16),
         pltpu.VMEM((2, 2 * n_slots, n_rows), bf16),
         pltpu.VMEM((2, n_rows, 2 * n_slots), bf16),
-        pltpu.VMEM((2, n_coarse + 2 * n_slots, total_coarse), bf16),
+        pltpu.VMEM((2, 2, n_coarse + 2 * n_slots, total_coarse // 2), bf16),
         pltpu.VMEM((n_sub, 2 * per_peer, total_coarse), f32),
         pltpu.VMEM((n_sub, 2 * per_peer, total_coarse), f32),
         pltpu.VMEM((n_sub, per_peer, n_rhs), f32),

time: 53.3 us -> 52.7 us (0.989)
    pallas_call x1, Pallas kernels: 50.6 us -> 50.1 us  [local(): pl.pallas_call(functools.partial(kernel, n_group, n_sub), out_shape=field...]
where the time goes in v4:
time: 52.7 us; the launch traced here: 52.6 us
  Pallas kernels  50.1 us (95%)
  local copies, waits for them, and re-layouts  1.85 us (4%)
  between operations  0.64 us (1%)
    pallas_call x1, Pallas kernels, local(): pl.pallas_call(functools.partial(kernel, n_group, n_sub), out_shape=field...  50.1 us
    squeeze x1, local copies, waits for them, and re-layouts, local(): return (both[0], both[1])  1.85 us

profile of v4, /device:TPU:0, one launch (start us, length us, event | category | flops | bytes accessed | tf_op | source)
XLA Modules:
  0.0 52.6 jit_solution(4510857188311516916)
XLA Ops:
  0.6 50.1 %shard_map.122 = f32[2,512,128]{2,1,0:T(8,128)} custom-call(f32[512,128]{1,0:T(8,128)} %refs_0_.1, f32[1,512]{1,0:T(1,128)} %refs_1_.1, f32[512,512]{1,0:T(8,128)} %refs_2_.1, s32[8,8]{1,0:T(8,128)} %refs_3_.1, s32[1,64]{1,0:T(1,128)} %refs_4_.1, s32[1,64]{1,0:T(1,128)} %refs_5_.1, s32[1,8]{1,0:T(1,128)} %refs_6_.1, f32[1,64]{1,0:T(1,128)} %refs_7_.1, ...), custom_call_target="tpu_custom_call" | custom-call | tf_op jit(solution)/shard_map/pallas_call | solution.py:482
  50.7 1.9 %slice_bitcast_fusion = (f32[512,128]{1,0:T(8,128)}, f32[512,128]{1,0:T(8,128)}) fusion(f32[2,512,128]{2,1,0:T(8,128)} %shard_map.122), kind=kLoop, calls=%fused_computation | loop fusion | bytes 1048576 | tf_op jit(solution)/shard_map/squeeze | solution.py:492

commit v5 on v4

--- a/solution.py
+++ b/solution.py
@@ -127,6 +127,7 @@
         pl.semaphore_signal(barrier, inc=1, device_id=(me_g, peer), device_id_type=MESH)
 
     sent = []
+    far_first = sorted(range(1, n_sub), key=lambda step: abs(step - n_sub // 2))
 
     def send(src, dst, channel, arrived, peer):
         pltpu.make_async_remote_copy(
@@ -139,7 +140,7 @@
         ).start()
 
     def over_sub(channel, src_of, dst, arrived_of=None):
-        for step in range(1, n_sub):
+        for step in far_first:
             peer = lax.rem(me_s + step, n_sub)
             arrived = recv_sem.at[channel] if arrived_of is None else arrived_of(step)
             send(src_of(peer), dst, channel, arrived, (me_g, peer))
@@ -309,7 +310,7 @@
                 extend_in[...].reshape(2 * n_slots, total_coarse),
                 slice(n_coarse, n_coarse + 2 * n_slots),
             )
-        for step in range(1, n_sub):
+        for step in reversed(far_first):
             origin = lax.rem(me_s + n_sub - step, n_sub)
             part = sub_buf.at[phase, core, origin, message(phase)]
             pltpu.make_async_copy(part, part, step_sem.at[phase, step]).wait()
@@ -435,6 +436,16 @@
 
     for channel, part in sent:
         pltpu.make_async_copy(part, part, send_sem.at[channel]).wait()
+
+
+def divide(both_ref, x_ref, r_ref, sem):
+    copies = [
+        pltpu.make_async_copy(both_ref.at[i], out, sem.at[i]) for i, out in enumerate((x_ref, r_ref))
+    ]
+    for copy in copies:
+        copy.start()
+    for copy in copies:
+        copy.wait()
 
 
 def local(n_group, n_sub, *args):
@@ -489,7 +500,16 @@
             collective_id=0, has_side_effects=True, vmem_limit_bytes=56 * 1024 * 1024
         ),
     )(*args)
-    return both[0], both[1]
+    half = jax.ShapeDtypeStruct((n_rows, n_rhs), f32)
+    anywhere = pl.BlockSpec(memory_space=pl.ANY)
+    return pl.pallas_call(
+        divide,
+        out_shape=(half, half),
+        in_specs=[anywhere],
+        out_specs=(anywhere, anywhere),
+        scratch_shapes=[pltpu.SemaphoreType.DMA((2,))],
+        compiler_params=pltpu.CompilerParams(vmem_limit_bytes=56 * 1024 * 1024),
+    )(both)
 
 
 def solution(mesh):

time: 52.7 us -> 67.8 us (1.29)
  Pallas kernels: 50.1 us -> 67.1 us
  local copies, waits for them, and re-layouts: 1.85 us -> 0 us
    pallas_call x0 -> x1, Pallas kernels: none -> 17 us  [local(): pl.pallas_call(divide, out_shape=(half, half), in_specs=[anywhere], out_s...]
    squeeze x1 -> x0, local copies, waits for them, and re-layouts: 1.85 us -> none  [local(): return (both[0], both[1])]
where the time goes in v5:
time: 67.8 us; the launch traced here: 67.7 us
  Pallas kernels  67.1 us (99%)
    pallas_call x1, Pallas kernels, local(): pl.pallas_call(functools.partial(kernel, n_group, n_sub), out_shape=field...  50.1 us
    pallas_call x1, Pallas kernels, local(): pl.pallas_call(divide, out_shape=(half, half), in_specs=[anywhere], out_s...  17 us

profile of v5, /device:TPU:0, one launch (start us, length us, event | category | flops | bytes accessed | tf_op | source)
XLA Modules:
  0.0 67.7 jit_solution(2860363288606341763)
XLA Ops:
  0.6 50.1 %shard_map.122.both_ref = f32[2,512,128]{2,1,0:T(8,128)} custom-call(f32[512,128]{1,0:T(8,128)} %refs_0_.1, f32[1,512]{1,0:T(1,128)} %refs_1_.1, f32[512,512]{1,0:T(8,128)} %refs_2_.1, s32[8,8]{1,0:T(8,128)} %refs_3_.1, s32[1,64]{1,0:T(1,128)} %refs_4_.1, s32[1,64]{1,0:T(1,128)} %refs_5_.1, s32[1,8]{1,0:T(1,128)} %refs_6_.1, f32[1,64]{1,0:T(1,128)} %refs_7_.1, ...), custom_call_target="tpu_custom_call" | custom-call | tf_op jit(solution)/shard_map/pallas_call | solution.py:493
  50.7 17.0 %shard_map.123 = (f32[512,128]{1,0:T(8,128)}, f32[512,128]{1,0:T(8,128)}) custom-call(f32[2,512,128]{2,1,0:T(8,128)} %shard_map.122.both_ref), custom_call_target="tpu_custom_call" | custom-call | tf_op jit(solution)/shard_map/pallas_call | solution.py:505

commit v6 on v4

--- a/solution.py
+++ b/solution.py
@@ -127,6 +127,7 @@
         pl.semaphore_signal(barrier, inc=1, device_id=(me_g, peer), device_id_type=MESH)
 
     sent = []
+    far_first = sorted(range(1, n_sub), key=lambda step: abs(step - n_sub // 2))
 
     def send(src, dst, channel, arrived, peer):
         pltpu.make_async_remote_copy(
@@ -139,7 +140,7 @@
         ).start()
 
     def over_sub(channel, src_of, dst, arrived_of=None):
-        for step in range(1, n_sub):
+        for step in far_first:
             peer = lax.rem(me_s + step, n_sub)
             arrived = recv_sem.at[channel] if arrived_of is None else arrived_of(step)
             send(src_of(peer), dst, channel, arrived, (me_g, peer))
@@ -309,7 +310,7 @@
                 extend_in[...].reshape(2 * n_slots, total_coarse),
                 slice(n_coarse, n_coarse + 2 * n_slots),
             )
-        for step in range(1, n_sub):
+        for step in reversed(far_first):
             origin = lax.rem(me_s + n_sub - step, n_sub)
             part = sub_buf.at[phase, core, origin, message(phase)]
             pltpu.make_async_copy(part, part, step_sem.at[phase, step]).wait()

time: 52.7 us -> 52.7 us (level)
  no operation moved by 1% of the time
where the time goes in v6:
time: 52.7 us; the launch traced here: 52.5 us
  Pallas kernels  50.1 us (95%)
  local copies, waits for them, and re-layouts  1.85 us (4%)
  between operations  0.64 us (1%)
    pallas_call x1, Pallas kernels, local(): pl.pallas_call(functools.partial(kernel, n_group, n_sub), out_shape=field...  50.1 us
    squeeze x1, local copies, waits for them, and re-layouts, local(): return (both[0], both[1])  1.85 us

profile of v6, /device:TPU:0, one launch (start us, length us, event | category | flops | bytes accessed | tf_op | source)
XLA Modules:
  0.0 52.5 jit_solution(17940987594906531997)
XLA Ops:
  0.6 50.1 %shard_map.122 = f32[2,512,128]{2,1,0:T(8,128)} custom-call(f32[512,128]{1,0:T(8,128)} %refs_0_.1, f32[1,512]{1,0:T(1,128)} %refs_1_.1, f32[512,512]{1,0:T(8,128)} %refs_2_.1, s32[8,8]{1,0:T(8,128)} %refs_3_.1, s32[1,64]{1,0:T(1,128)} %refs_4_.1, s32[1,64]{1,0:T(1,128)} %refs_5_.1, s32[1,8]{1,0:T(1,128)} %refs_6_.1, f32[1,64]{1,0:T(1,128)} %refs_7_.1, ...), custom_call_target="tpu_custom_call" | custom-call | tf_op jit(solution)/shard_map/pallas_call | solution.py:483
  50.7 1.9 %slice_bitcast_fusion = (f32[512,128]{1,0:T(8,128)}, f32[512,128]{1,0:T(8,128)}) fusion(f32[2,512,128]{2,1,0:T(8,128)} %shard_map.122), kind=kLoop, calls=%fused_computation | loop fusion | bytes 1048576 | tf_op jit(solution)/shard_map/squeeze | solution.py:493
